TPU v7x, 32 devices: a whole 2x2x4 slice. The times are simulated.
32 devices in a mesh: wide: 8 (over z, x), narrow: 4 (over y, core).
Axes of the slice: x: 2, y: 2, z: 4, core: 2. Of those that a mesh axis runs over, the one named last changes fastest.
Arguments:
- views: bfloat16 [128, 7, 7, 2048], P('wide', None, None, 'narrow'), may hold values from -6 to 6
- crops: bfloat16 [256, 3, 3, 2048], P('wide', None, None, 'narrow'), may hold values from -6 to 6
- image_count: int32 [8], P('wide'), may hold values from 2 to 8, as said below
- w_reduce: bfloat16 [2048, 512], P(None, 'narrow'), may hold values from -0.125 to 0.125
- w_spatial: bfloat16 [3, 3, 512, 512], P(None, None, 'narrow'), may hold values from -0.09375 to 0.09375
- w_expand: bfloat16 [512, 2048], P('narrow'), may hold values from -0.25 to 0.25
- gain_one: float32 [512], P('narrow'), may hold values from 0.5 to 1.5
- shift_one: float32 [512], P('narrow'), may hold values from -3 to 3
- gain_two: float32 [512], P('narrow'), may hold values from 0.5 to 1.5
- shift_two: float32 [512], P('narrow'), may hold values from -3 to 3
- gain_three: float32 [2048], P('narrow'), may hold values from 0.5 to 1.5
- shift_three: float32 [2048], P('narrow'), may hold values from -3 to 3
- view_cotangent: bfloat16 [128, 7, 7, 2048], P('wide', None, None, 'narrow'), may hold values from -6 to 6
- crop_cotangent: bfloat16 [256, 3, 3, 2048], P('wide', None, None, 'narrow'), may hold values from -6 to 6
Outputs:
- view_result: bfloat16 [128, 7, 7, 2048], P('wide', None, None, 'narrow')
- crop_result: bfloat16 [256, 3, 3, 2048], P('wide', None, None, 'narrow')
- view_gradient: bfloat16 [128, 7, 7, 2048], P('wide', None, None, 'narrow')
- crop_gradient: bfloat16 [256, 3, 3, 2048], P('wide', None, None, 'narrow')
- reduce_gradient: float32 [2048, 512], P(None, 'narrow')
- spatial_gradient: float32 [3, 3, 512, 512], P(None, None, 'narrow')
- expand_gradient: float32 [512, 2048], P('narrow')
- gain_one_grad: float32 [512], P('narrow')
- shift_one_grad: float32 [512], P('narrow')
- gain_two_grad: float32 [512], P('narrow')
- shift_two_grad: float32 [512], P('narrow')
- gain_three_grad: float32 [2048], P('narrow')
- shift_three_grad: float32 [2048], P('narrow')
Inputs may be any that keep to these rules, and one draw needn't show every extreme that they name: image_count[d] real images among the 8 slots of wide index d, the later slots being padding; in every draw some index has all 8.
All inputs are finite; a program needn't handle non-finite values.
Results may differ from a plain program's by a relative error of at most 0.013.
Values may be sent and summed in bfloat16 or wider, within the bound.
A program may use at most 128 MiB of HBM per device.

v0:
```python
import functools

import jax
import jax.numpy as jnp
from jax import lax
from jax.experimental import pallas as pl
from jax.experimental.pallas import tpu as pltpu
from jax.sharding import PartitionSpec as P

MESH = pl.DeviceIdType.MESH
EPS = 1e-05
ORDER = (
    ('e', 's0', 's2', 'e'),
    ('s2', 's1'),
    ('s3', 's2', 's0', 'e'),
    ('r0', 'r1', 's3', 's1', 's0', 's2', 's3', 'e', 'r0', 'r1', 's2', 's0', 's1', 's3', 'e', 's3', 'r0', 's1', 's2', 'r1', 's3', 'r0', 'r1'),
)
WAYS = {"e": "d", "s0": "q", "s1": "q", "s2": "z", "s3": "z", "r0": "q", "r1": "q"}
NARROW = 4
CHUNKS = 2
COPIES = 75
ROW_TILE = 16
GROUP = 8
VIEWS_EACH = 2
CROPS_EACH = 4
TAPS = [(i, j) for i in range(3) for j in range(3)]
XOR = (0, 2, 1, 3)
POS = (0, 2, 1, 3)
F32 = jnp.float32
BF16 = jnp.bfloat16


def dot(a, b):
    return jnp.dot(a, b, preferred_element_type=F32)


def dot_right(a, b):
    return lax.dot_general(a, b, (((1,), (1,)), ((), ())), preferred_element_type=F32)


def dot_left(a, b):
    return lax.dot_general(a, b, (((0,), (0,)), ((), ())), preferred_element_type=F32)


def logistic(v):
    return 0.5 + 0.5 * jnp.tanh(0.5 * v)


def flip(index, bit):
    return index + bit - 2 * bit * ((index // bit) % 2)


def wider(tile, lanes):
    return jnp.concatenate([tile] * (lanes // 128), axis=1) if lanes > 128 else tile


def fold(v):
    return jnp.sum(v.reshape(v.shape[0] // 8, 8, v.shape[1]), axis=0)


def total(v):
    return jnp.sum(v, axis=0, keepdims=True)


def flat(v):
    return jnp.concatenate([v[k : k + 1] for k in range(v.shape[0])], axis=1)


class Links:
    def __init__(self, send_sems, recv_sems):
        self.send_sems, self.recv_sems, self.used, self.sent = send_sems, recv_sems, 0, []

    def send(self, source, target, peer, background=""):
        copy = pltpu.make_async_remote_copy(
            source,
            target,
            self.send_sems.at[self.used],
            self.recv_sems.at[self.used],
            device_id=peer,
            device_id_type=MESH,
        )
        self.used += 1
        copy.start()
        self.sent.append(copy)
        return copy

    def settle(self, copy):
        if any(other is copy for other in self.sent):
            copy.wait_send()
            self.sent = [other for other in self.sent if other is not copy]


class Group:
    def __init__(self, links, copies, total, kind):
        self.live = True
        send_sem, recv_sem = links.send_sems.at[links.used], links.recv_sems.at[links.used]
        links.used += 1
        for source, target, peer in copies:
            copy = pltpu.make_async_remote_copy(
                source, target, send_sem, recv_sem, device_id=peer, device_id_type=MESH
            )
            copy.start()
        self.arrival = pltpu.make_async_copy(total, total, recv_sem)
        self.departure = pltpu.make_async_copy(total, total, send_sem)
        links.sent.append(self)

    def wait_recv(self):
        if self.live:
            self.arrival.wait()

    def wait_send(self):
        self.departure.wait()


def kernel(wide, dims, *refs):
    views_side, views_block, crops_side, crops_block, rows, padded = dims
    (
        image_count, views, crops, view_cot, crop_cot, w_reduce, w_spatial, w_expand,
        gain1, shift1, gain2, shift2, gain3, shift3,
        view_out, crop_out, view_grad, crop_grad, reduce_out, spatial_out, expand_out, small_out, large_out,
        count_ref, inner_vectors, outer_vectors, small, large,
        x, xs, cot, wr, ws, we, mask, stat, stat_all, keep, near_out, near_in, far_out, far_in,
        red, mix, back, view_pad, crop_pad, taps, mall, ht, b3, ge, gall, gm, tp, gr, res, dx,
        out_e, out_s, out_r, stage_e, part_e, came_e,
        part_s, came_s, part_r, came_r,
        send_sems, recv_sems, stat_send, stat_recv, local_sems,
    ) = refs
    w = lax.axis_index("wide")
    q = lax.axis_index("narrow")
    near, far = (w, flip(q, 1)), (w, flip(q, 2))
    inner = w_reduce.shape[1]
    own = x.shape[1]
    full = NARROW * inner
    chunk = padded // CHUNKS
    half = 2 * inner
    nview = views.shape[0]
    group = min(wide, GROUP)
    ex = tp.at[:, pl.ds(0, own)]
    links = Links(send_sems, recv_sems)
    slot = [0]

    def local(source, target):
        copy = pltpu.make_async_copy(source, target, local_sems.at[slot[0]])
        slot[0] += 1
        copy.start()
        return copy

    def part(r):
        return pl.ds(r * chunk, chunk)

    def lanes(p, width=inner):
        return pl.ds(p * width, width)

    def dyn_lanes(p, width=inner):
        return pl.ds(pl.multiple_of(p * width, width), width)

    def narrow_peer(p):
        i = q
        if XOR[p] & 1:
            i = flip(i, 1)
        if XOR[p] & 2:
            i = flip(i, 2)
        return i

    def loop(body, init):
        return lax.fori_loop(
            0, CHUNKS, lambda i, c: body(pl.ds(pl.multiple_of(i * chunk, chunk), chunk), c), init
        )

    def own_rows(p):
        return pl.ds(pl.multiple_of(narrow_peer(p) * own, own), own)

    load_count = local(image_count, count_ref)
    load_vectors = [local(ref, inner_vectors.at[k]) for k, ref in enumerate((gain1, shift1, gain2, shift2))]
    load_vectors += [local(ref, outer_vectors.at[k]) for k, ref in enumerate((gain3, shift3))]
    load_reduce = [local(w_reduce.at[own_rows(2 * k), :], wr.at[k, :, lanes(0)]) for k in range(2)]
    load_x = [local(views, x.at[pl.ds(0, nview)]), local(crops, x.at[pl.ds(nview, rows - nview)])]
    load_spatial = [
        local(w_spatial.at[:, dyn_lanes(narrow_peer(p))], ws.at[:, lanes(p)]) for p in range(NARROW)
    ]
    own_expand = local(w_expand.at[:, dyn_lanes(q, own)], we.at[lanes(0), :])
    load_cot = [
        local(view_cot, cot.at[pl.ds(0, nview)]), local(crop_cot, cot.at[pl.ds(nview, rows - nview)])
    ]
    barrier = pltpu.get_barrier_semaphore()

    def greet(k, c):
        pl.semaphore_signal(
            barrier,
            inc=1,
            device_id=(lax.rem(w + k % wide, wide), lax.rem(q + k // wide, NARROW)),
            device_id_type=MESH,
        )
        return c

    everyone = NARROW * wide - 1
    lax.fori_loop(1, everyone + 1, greet, 0, unroll=wide <= 16)

    load_count.wait()
    real = count_ref[0]
    row = lax.broadcasted_iota(jnp.int32, (chunk, 128), 0)
    for r in range(CHUNKS):
        at = row + r * chunk
        image = jnp.where(
            at < nview,
            (at % views_block) // VIEWS_EACH,
            ((at - nview) % crops_block) // CROPS_EACH,
        )
        alive = jnp.where((image < real) & (at < rows), 1.0, 0.0)
        mask[part(r)] = alive.astype(F32)
    tail = pl.ds(rows, padded - rows)
    x[tail] = jnp.zeros((padded - rows, own), BF16)
    xs[1, tail] = jnp.zeros((padded - rows, own), BF16)
    cot[tail] = jnp.zeros((padded - rows, own), BF16)
    taps[tail] = jnp.zeros((padded - rows, len(TAPS) * inner), BF16)
    view_pad[...] = jnp.zeros(view_pad.shape, BF16)
    crop_pad[...] = jnp.zeros(crop_pad.shape, BF16)
    my_count = real.astype(F32) * float(
        VIEWS_EACH * views_side**2 + CROPS_EACH * crops_side**2
    )

    pl.semaphore_wait(barrier, everyone)

    far_reduce = [
        links.send(w_reduce.at[own_rows(1 + 2 * k), :], wr.at[k, :, lanes(1)], far) for k in range(2)
    ]
    near_x = [
        links.send(views, xs.at[1, pl.ds(0, nview)], near),
        links.send(crops, xs.at[1, pl.ds(nview, rows - nview)], near),
    ]
    near_reduce = [links.send(w_reduce.at[own_rows(2), :], wr.at[0, :, lanes(2)], near)]

    def exchange(k, tile, everywhere=False):
        board, me, n = (stat_all, q * wide + w, everyone) if everywhere else (stat, w, wide - 1)
        sem = k + 4 if everywhere else k
        board[k, me] = tile

        def put(step, c):
            pltpu.make_async_remote_copy(
                board.at[k, me],
                board.at[k, me],
                stat_send.at[sem],
                stat_recv.at[sem],
                device_id=(lax.rem(w + step % wide, wide), lax.rem(q + step // wide, NARROW)),
                device_id_type=MESH,
            ).start()
            return c

        lax.fori_loop(1, n + 1, put, 0, unroll=wide <= 16)
        several = board.at[k, pl.ds(0, n)]
        pending.append(pltpu.make_async_copy(several, several, stat_send.at[sem]))
        return pltpu.make_async_copy(several, several, stat_recv.at[sem])

    pending = []

    def moments(ref):
        size = ref.shape[1]
        zero = jnp.zeros((8, size), F32)
        sums = total(loop(lambda at, c: c + fold(ref[at, :] * wider(mask[at, :], size)), zero))
        center = sums / my_count
        squares = total(
            loop(
                lambda at, c: c + fold(jnp.square(ref[at, :] - center) * wider(mask[at, :], size)),
                zero,
            )
        )
        return sums, squares

    def rows_of(k, lo, n):
        return stat[k, :, pl.ds(lo, n), :]

    def combine(sums, squares, counts, pixels):
        center = jnp.sum(sums, axis=0) / pixels
        spread = (
            jnp.sum(squares + counts * jnp.square(sums / counts - center[None]), axis=0) / pixels
        )
        return center, lax.rsqrt(spread + EPS)

    def reduce_scatter(k, give, hold, target, after, meanwhile=lambda: None):
        first, second = [], []
        for copy in in_use.pop(k, ()):
            links.settle(copy)
        for r in range(CHUNKS):
            near_out[k, part(r)] = give(r).astype(BF16)
            first.append(links.send(near_out.at[k, part(r)], near_in.at[k, part(r)], near))
        for r in range(CHUNKS):
            keep[part(r)] = hold(r)
            first[r].wait_recv()
            far_out[k, part(r)] = (
                keep[part(r), lanes(1)] + near_in[k, part(r), lanes(1)].astype(F32)
            ).astype(BF16)
            second.append(links.send(far_out.at[k, part(r)], far_in.at[k, part(r)], far))
            target[part(r)] = keep[part(r), lanes(0)] + near_in[k, part(r), lanes(0)].astype(F32)
        meanwhile()
        for r in range(CHUNKS):
            second[r].wait_recv()
            target[part(r)] = target[part(r)] + far_in[k, part(r)].astype(F32)
            after(r)
        in_use[k] = first + second

    in_use = {}

    class Gather:
        def __init__(self, ref):
            self.ref, self.across, self.onward = ref, [], []

        def send(self, r):
            ref = self.ref
            self.across.append(links.send(ref.at[part(r), lanes(0)], ref.at[part(r), lanes(1)], far))
            if r == CHUNKS - 1:
                self.straight = links.send(ref.at[:, lanes(0)], ref.at[:, lanes(2)], near)

        def hand_on(self, count):
            for r in range(len(self.onward), min(len(self.onward) + count, CHUNKS)):
                self.across[r].wait_recv()
                self.onward.append(
                    links.send(self.ref.at[part(r), lanes(1)], self.ref.at[part(r), lanes(3)], near)
                )

        def near_end(self):
            if self.straight is not None:
                self.straight.wait_recv()
                self.straight = None

        def end(self, use):
            for r in range(CHUNKS + 1):
                self.hand_on(1)
                if r > 0:
                    self.near_end()
                    self.onward[r - 1].wait_recv()
                    use(r - 1)

    across_x, onward_x, shared = [], [], [0]

    def share_x(eighths):
        low = shared[0]
        shared[0] = low + eighths
        first, last = (padded // ROW_TILE * k // 8 * ROW_TILE for k in (low, shared[0]))
        at = pl.ds(first, last - first)
        across_x.append((at, links.send(x.at[at], xs.at[0, at], far, "x")))

    def share_end():
        while len(onward_x) < len(across_x):
            at, copy = across_x[len(onward_x)]
            copy.wait_recv()
            onward_x.append(links.send(xs.at[0, at], xs.at[2, at], near, "x"))

    group_start = w - lax.rem(w, group)

    def block_of(bits, index):
        return sum((index // bit) % 2 * (group // 2 >> k) for k, bit in enumerate(bits))

    def beyond(value, spare):
        bit, at = group, group
        while bit < wide:
            spare[at] = value.astype(BF16)
            copy = links.send(spare.at[at], spare.at[at + 1], (flip(w, bit), q))
            copy.wait_recv()
            value = spare[at].astype(F32) + spare[at + 1].astype(F32)
            bit, at = bit * 2, at + 2
        return value

    def add_block(parts, at, came):
        parts[at] = (parts[at].astype(F32) + came.astype(F32)).astype(BF16)

    def halved(kind, bits, parts, came, finish):
        low, size = 0, group
        for bit in bits:
            size //= 2
            side = (w // bit) % 2
            box = pl.ds(group - 2 * size, size)
            copy = links.send(
                parts.at[pl.ds(low + (1 - side) * size, size)], came.at[box], (flip(w, bit), q), kind
            )
            yield
            copy.wait_recv()
            low = low + side * size
            if size > 1:
                for k in range(size):
                    add_block(parts, low + k, came[group - 2 * size + k])
        value = parts[low].astype(F32) + came[group - 2].astype(F32)
        yield from finish(beyond(value, came))

    def doubled(kind, bits, out):
        low, size = block_of(bits, w), 1
        for bit in reversed(bits):
            box = pl.ds(low, size)
            copy = links.send(out.at[box], out.at[box], (flip(w, bit), q), kind)
            yield
            copy.wait_recv()
            low = low - (w // bit) % 2 * size
            size *= 2

    def group_peers(among):
        for k in range(1, len(among)):
            place = (lax.rem(w, group) + k * (among[1] - among[0])) % group
            yield (group_start + place, q), place

    def halved_then_direct(kind, bits, parts, came, finish):
        quads = group // 2
        side = (w // bits[0]) % 2
        copy = links.send(
            parts.at[pl.ds((1 - side) * quads, quads)], came.at[pl.ds(0, quads)], (flip(w, bits[0]), q), kind
        )
        yield
        copy.wait_recv()
        for k in range(quads):
            add_block(parts, side * quads + k, came[k])
        mine = block_of(bits, w)
        copy = Group(
            links,
            [
                (parts.at[block_of(bits, place)], came.at[quads + mine % quads], peer)
                for peer, place in group_peers(range(0, group, 2))
            ],
            came.at[pl.ds(quads, quads - 1)],
            kind,
        )
        came[quads + mine % quads] = parts[mine]
        yield
        copy.wait_recv()
        value = jnp.sum(came[pl.ds(quads, quads)].astype(F32), axis=0)
        yield from finish(beyond(value, came))

    def direct_then_doubled(kind, bits, out):
        mine = block_of(bits, w)
        copy = Group(
            links,
            [(out.at[mine], out.at[mine], peer) for peer, _ in group_peers(range(0, group, 2))],
            out.at[pl.ds(0, group // 2 - 1)],
            kind,
        )
        yield
        copy.wait_recv()
        box = pl.ds((w // bits[0]) % 2 * (group // 2), group // 2)
        copy = links.send(out.at[box], out.at[box], (flip(w, bits[0]), q), kind)
        yield
        copy.wait_recv()

    def direct(kind, bits, parts, came, finish):
        mine = block_of(bits, w)
        copy = Group(
            links,
            [
                (parts.at[block_of(bits, place)], came.at[mine], peer)
                for peer, place in group_peers(range(group))
            ],
            came.at[pl.ds(0, group - 1)],
            kind,
        )
        came[mine] = parts[mine]
        yield
        copy.wait_recv()
        value = jnp.sum(came[pl.ds(0, group)].astype(F32), axis=0)
        yield from finish(beyond(value, came))

    ways = {
        "h": ((1, 2, 4), halved, doubled),
        "z": ((2, 1, 4), halved, doubled),
        "q": ((1, 2, 4), halved_then_direct, direct_then_doubled),
        "d": ((1, 2, 4), direct, doubled),
    }

    def all_reduced(kind, way, parts, came, out, keep_sum, between=lambda: iter(())):
        bits, there, back = ways[way]

        def finish(value):
            keep_sum(block_of(bits, w), value)
            yield from between()
            yield from back(kind, bits, out)

        return there(kind, bits, parts, came, finish)

    tasks = {}

    def begin(name, task):
        tasks[name] = task
        next(task)

    def advance(*names):
        for name in names:
            if name in tasks and next(tasks[name], "end") == "end":
                del tasks[name]

    for copy in load_reduce + load_x:
        copy.wait()
    for copy in near_x:
        copy.wait_recv()

    def reduce_part(r, p):
        return dot(x[part(r)], wr[0, :, lanes(p)]) + dot(xs[1, part(r)], wr[1, :, lanes(p)])

    for r in range(CHUNKS):
        red[part(r)] = reduce_part(r, 0)
    for copy in far_reduce:
        copy.wait_recv()
    came = []
    for r in range(CHUNKS):
        far_out[0, part(r)] = reduce_part(r, 1).astype(BF16)
        came.append(links.send(far_out.at[0, part(r)], far_in.at[0, part(r)], far))
    near_reduce.append(links.send(wr.at[1, :, lanes(1)], wr.at[0, :, lanes(3)], near))
    for r in range(CHUNKS):
        came[r].wait_recv()
        red[part(r)] = red[part(r)] + far_in[0, part(r)].astype(F32)
    in_use[0] = came
    sent_expand = {
        p: links.send(
            w_expand.at[:, dyn_lanes(narrow_peer(p), own)], we.at[lanes(p), :], (w, narrow_peer(p))
        )
        for p in (3, 1, 2)
    }
    share_x(1)
    sums, squares = moments(red)
    arrived = exchange(
        0,
        jnp.concatenate(
            [sums, squares, jnp.full((1, inner), my_count, F32), jnp.zeros((5, inner), F32)], axis=0
        ),
    )
    for copy in load_spatial:
        copy.wait()
    arrived.wait()
    counts = rows_of(0, 2, 1)
    pixels = jnp.sum(counts, axis=0)
    center1, inverse1 = combine(rows_of(0, 0, 1), rows_of(0, 1, 1), counts, pixels)

    def normed(v, center, inverse, gain, shift):
        standard = (v - center) * inverse
        return standard, gain * standard + shift

    for copy in load_vectors:
        copy.wait()
    g1, s1, g2, s2 = (inner_vectors[k] for k in range(4))
    g3, s3 = (outer_vectors[k] for k in range(2))
    grids = (
        (views_side, views_block, 0, view_pad),
        (crops_side, crops_block, nview, crop_pad),
    )
    for side, block, lead, pad in grids:
        line = side * block
        for h in range(side):
            _, v = normed(red[pl.ds(lead + h * line, line)], center1, inverse1, g1, s1)
            pad[pl.ds(((h + 1) * (side + 2) + 1) * block, line)] = (v * logistic(v)).astype(BF16)
    for side, block, lead, pad in grids:
        line = side * block
        for t, (i, j) in enumerate(TAPS):
            for h in range(side):
                taps[pl.ds(lead + h * line, line), lanes(t)] = pad[
                    pl.ds(((h + i) * (side + 2) + j) * block, line)
                ]

    mixes = Gather(mall)
    reference = []

    def send_mix(r):
        if r == 0:
            alive = mask[part(0)]
            reference.append(total(fold(mix[part(0)] * alive)) / total(fold(alive)))
        mall[part(r), lanes(0)] = (mix[part(r)] - reference[0]).astype(BF16)
        mixes.send(r)

    reduce_scatter(
        1,
        lambda r: dot(taps[part(r)], ws[:, pl.ds(half, half)]),
        lambda r: dot(taps[part(r)], ws[:, pl.ds(0, half)]),
        mix,
        send_mix,
    )
    sums, squares = moments(mix)
    arrived = exchange(
        0,
        jnp.concatenate([sums, squares, g2, s2, reference[0], jnp.zeros((3, inner), F32)], axis=0),
        True,
    )
    own_expand.wait()
    for p in (2, 3, 1):
        sent_expand[p].wait_recv()
    mixes.hand_on(CHUNKS)
    arrived.wait()

    def board_rows(k, p, lo, n):
        return stat_all[k, pl.ds(narrow_peer(p) * wide, wide), pl.ds(lo, n), :]

    def board_row(k, p, lo):
        return stat_all[k, narrow_peer(p) * wide + w, pl.ds(lo, 1), :]

    blocks = [
        combine(board_rows(0, p, 0, 1), board_rows(0, p, 1, 1), counts, pixels) for p in range(NARROW)
    ]
    center2, inverse2 = blocks[0]
    inverse_all = jnp.concatenate([b[1] for b in blocks], axis=1)
    offset_all = jnp.concatenate(
        [board_row(0, p, 4) - blocks[p][0] for p in range(NARROW)], axis=1
    )
    gain_all = jnp.concatenate([board_row(0, p, 2) for p in range(NARROW)], axis=1)
    shift_all = jnp.concatenate([board_row(0, p, 3) for p in range(NARROW)], axis=1)
    scale_all = gain_all * inverse_all
    constant_all = scale_all * offset_all + shift_all

    def expand(r):
        v = mall[part(r), :].astype(F32) * scale_all + constant_all
        ht[part(r), :] = (v * logistic(v)).astype(BF16)
        ex[part(r), :] = dot(ht[part(r)], we[...])

    mixes.end(expand)
    share_end()
    share_x(5)
    sums, squares = moments(ex)
    groups = own // 128

    def tiles(*values):
        return jnp.concatenate(
            [v[:, 128 * k : 128 * k + 128] for v in values for k in range(groups)], axis=0
        )

    arrived = exchange(1, tiles(sums, squares))
    for copy in load_cot:
        copy.wait()
    arrived.wait()
    center3, inverse3 = combine(
        rows_of(1, 0, groups), rows_of(1, groups, groups), counts, pixels
    )
    center3, inverse3 = flat(center3), flat(inverse3)

    def third(at, c):
        standard, v = normed(ex[at, :], center3, inverse3, g3, s3)
        v = v + x[at].astype(F32)
        s = logistic(v)
        alive = wider(mask[at], own)
        res[at] = (alive * (v * s)).astype(BF16)
        g = cot[at].astype(F32) * alive * (s * (1.0 + v * (1.0 - s)))
        b3[at] = g
        return c[0] + fold(g), c[1] + fold(g * standard)

    zero = jnp.zeros((8, own), F32)
    shift_sum, gain_sum = loop(third, (zero, zero))
    arrived = exchange(2, tiles(total(gain_sum), total(shift_sum)))
    results = [
        local(res.at[pl.ds(0, nview)], view_out), local(res.at[pl.ds(nview, rows - nview)], crop_out)
    ]
    arrived.wait()
    both = jnp.sum(stat[2], axis=0)
    large[...] = both
    results.append(local(large, large_out))

    def back_terms(gain_grad, shift_grad, offset, inverse, gain, n):
        scale = gain * inverse
        slope = scale * inverse * (gain_grad / n)
        return scale, scale * (shift_grad / n) + slope * offset, slope

    scale3, base3, slope3 = back_terms(
        flat(both[:groups]), flat(both[groups:]), -center3, inverse3, g3, wider(pixels, own)
    )

    def third_back(at, c):
        ge[at] = (
            scale3 * b3[at] - wider(mask[at], own) * (base3 + slope3 * ex[at, :])
        ).astype(BF16)
        return c

    loop(third_back, 0)

    size_e = inner // group

    def keep_e(mine, value):
        stage_e[...] = value.astype(BF16)
        out_e[mine, :, dyn_lanes(q, own)] = stage_e[0]

    def hand_on_e():
        mine = block_of(ways[WAYS["e"]][0], w)
        got = [
            links.send(
                stage_e.at[p], out_e.at[mine, :, dyn_lanes(q, own)], (w, narrow_peer(p)), "e"
            )
            for p in range(1, NARROW)
        ]
        yield
        for copy in got:
            copy.wait_recv()

    def expand_gradient():
        value = dot_left(ht[...], ge[...]).astype(BF16)
        for p in range(NARROW):
            part_e[:, p] = value[inner * p : inner * (p + 1)].reshape(group, size_e, own)
        begin("e", all_reduced("e", WAYS["e"], part_e, came_e, out_e, keep_e, hand_on_e))
        share_end()

    def slope_of(v):
        s = logistic(v)
        return s * (1.0 + v * (1.0 - s))

    grads = Gather(gall)
    back_sums = [jnp.zeros((8, inner), F32)] * 2

    def second_back(r):
        standard, v = normed(mix[part(r)], center2, inverse2, g2, s2)
        g = back[part(r)] * slope_of(v)
        gall[part(r), lanes(0)] = g.astype(BF16)
        grads.send(r)
        back_sums[0] = back_sums[0] + fold(g * standard)
        back_sums[1] = back_sums[1] + fold(g)

    reduce_scatter(
        0,
        lambda r: dot_right(ge[part(r)], we[pl.ds(half, half), :]),
        lambda r: dot_right(ge[part(r)], we[pl.ds(0, half), :]),
        back,
        second_back,
        expand_gradient,
    )
    arrived = exchange(
        1,
        jnp.concatenate([*map(total, back_sums), jnp.zeros((6, inner), F32)], axis=0),
        True,
    )
    grads.hand_on(CHUNKS)
    arrived.wait()
    sums = [jnp.sum(board_rows(1, p, 0, 2), axis=0) for p in range(NARROW)]
    small[pl.ds(8, 8)] = jnp.concatenate([sums[0], jnp.zeros((6, inner), F32)], axis=0)
    scale2, base2, slope2 = back_terms(
        jnp.concatenate([v[0:1] for v in sums], axis=1),
        jnp.concatenate([v[1:2] for v in sums], axis=1),
        offset_all,
        inverse_all,
        gain_all,
        wider(pixels, full),
    )

    def columns(v, p, n=1):
        return v[:, inner * p : inner * (p + n)]

    def grad_mixed(at, some):
        for p in some:
            gm[at, lanes(p)] = (
                columns(scale2, p) * gall[at, lanes(p)].astype(F32)
                - mask[at] * (columns(base2, p) + columns(slope2, p) * mall[at, lanes(p)].astype(F32))
            ).astype(BF16)
        return 0

    def spatial_gradient(*some):
        value = dot_left(taps[...], jnp.concatenate([gm[:, lanes(p)] for p in some], axis=1))
        for k, p in enumerate(some):
            part_s[p] = columns(value, k).astype(BF16).reshape(part_s.shape[1:])

            def keep_s(mine, value, p=p):
                out_s[p, mine] = value.astype(BF16)

            name = "s%d" % p
            begin(
                name, all_reduced("s", WAYS[name], part_s.at[p], came_s.at[p], out_s.at[p], keep_s)
            )

    grads.near_end()
    loop(lambda at, c: grad_mixed(at, (0, 2)), 0)
    spatial_gradient(0, 2)
    advance("e")

    def spatial_back(r):
        grad_mixed(part(r), (1, 3))
        tp[part(r)] = dot_right(gm[part(r)], ws[...])

    grads.end(spatial_back)
    spatial_gradient(1, 3)
    share_x(2)
    shift_sum = gain_sum = jnp.zeros((8, inner), F32)
    for side, block, lead, pad in grids:
        line = side * block
        for h in range(side):
            g = None
            for t, (i, j) in enumerate(TAPS):
                source = h - (i - 1)
                if not 0 <= source < side:
                    continue
                first = lead + source * line
                if j == 1:
                    term = tp[pl.ds(first, line), lanes(t)]
                elif j == 0:
                    term = jnp.concatenate(
                        [tp[pl.ds(first + block, line - block), lanes(t)], jnp.zeros((block, inner), F32)]
                    )
                else:
                    term = jnp.concatenate(
                        [jnp.zeros((block, inner), F32), tp[pl.ds(first, line - block), lanes(t)]]
                    )
                g = term if g is None else g + term
            at = pl.ds(lead + h * line, line)
            standard, v = normed(red[at], center1, inverse1, g1, s1)
            g = g * slope_of(v)
            back[at] = g
            shift_sum = shift_sum + fold(g)
            gain_sum = gain_sum + fold(g * standard)
    back[tail] = jnp.zeros((padded - rows, inner), F32)
    arrived = exchange(
        3, jnp.concatenate([total(gain_sum), total(shift_sum), jnp.zeros((6, inner), F32)], axis=0)
    )

    advance(*ORDER[0])
    arrived.wait()
    both = jnp.sum(stat[3], axis=0)
    small[pl.ds(0, 8)] = both
    results.append(local(small, small_out))
    scale1, base1, slope1 = back_terms(both[0:1], both[1:2], -center1, inverse1, g1, pixels)

    def first_grad(at, c):
        gr[at, lanes(0)] = (scale1 * back[at] - mask[at] * (base1 + slope1 * red[at])).astype(BF16)
        return c

    loop(first_grad, 0)
    ends = Gather(gr)
    for r in range(CHUNKS):
        ends.send(r)

    per = own // 4

    def reduce_gradient(k):
        for p in (k, 2 + k):
            source = x[...] if p == 0 else xs[p - 1]
            value = dot_left(gr[:, lanes(0)], source).astype(BF16)
            for m in range(4):
                part_r[k, narrow_peer(p) % 2 * 4 + m] = value[:, per * m : per * m + per]

        def keep_r(mine, value):
            out_r[k, mine] = value.T.astype(BF16)

        name = "r%d" % k
        begin(name, all_reduced("r", WAYS[name], part_r.at[k], came_r.at[k], out_r.at[k], keep_r))

    reduce_gradient(0)
    advance(*ORDER[1])
    share_end()
    for copy in onward_x:
        copy.wait_recv()
    reduce_gradient(1)
    advance(*ORDER[2])

    def input_gradient(r):
        dx[part(r)] = (dot_right(gr[part(r)], wr[0]) + b3[part(r)]).astype(BF16)

    for copy in near_reduce:
        copy.wait_recv()
    ends.end(input_gradient)
    results += [
        local(dx.at[pl.ds(0, nview)], view_grad), local(dx.at[pl.ds(nview, rows - nview)], crop_grad)
    ]
    advance(*ORDER[3])
    results.append(local(out_e, expand_out))
    while tasks:
        advance(*list(tasks))
    results += [
        local(out_s.at[p], spatial_out.at[:, :, dyn_lanes(narrow_peer(p))]) for p in range(NARROW)
    ]
    chip = q // 2
    results += [local(out_r.at[0], reduce_out.at[chip]), local(out_r.at[1], reduce_out.at[1 - chip])]
    for copy in links.sent:
        copy.wait_send()
    for copy in pending:
        copy.wait()
    for copy in results:
        copy.wait()


def rows_first(a):
    return a.transpose(1, 2, 0, 3).reshape(-1, a.shape[3])


def images_first(a, like):
    n, h, w, c = like.shape
    return a.reshape(h, w, n, c).transpose(2, 0, 1, 3)


def per_device(wide, *args):
    (
        views, crops, image_count, w_reduce, w_spatial, w_expand,
        gain_one, shift_one, gain_two, shift_two, gain_three, shift_three, view_cot, crop_cot,
    ) = args
    own = views.shape[3]
    inner = w_reduce.shape[1]
    full = NARROW * inner
    nview = views.shape[0] * views.shape[1] * views.shape[2]
    ncrop = crops.shape[0] * crops.shape[1] * crops.shape[2]
    rows = nview + ncrop
    quantum = CHUNKS * ROW_TILE
    padded = -(-rows // quantum) * quantum
    dims = (views.shape[1], views.shape[0], crops.shape[1], crops.shape[0], rows, padded)
    ntaps = len(TAPS) * inner
    group = min(wide, GROUP)
    levels = (wide // group).bit_length() - 1
    slots = group + 2 * levels
    copies = COPIES + len(WAYS) * levels
    vm = pltpu.VMEM
    hbm = pl.BlockSpec(memory_space=pltpu.HBM)
    outs = pl.pallas_call(
        functools.partial(kernel, wide, dims),
        name="block",
        out_shape=(
            jax.ShapeDtypeStruct((nview, own), BF16),
            jax.ShapeDtypeStruct((ncrop, own), BF16),
            jax.ShapeDtypeStruct((nview, own), BF16),
            jax.ShapeDtypeStruct((ncrop, own), BF16),
            jax.ShapeDtypeStruct((2, group, own // 4, inner), BF16),
            jax.ShapeDtypeStruct((group, ntaps // group, full), BF16),
            jax.ShapeDtypeStruct((group, inner // group, NARROW * own), BF16),
            jax.ShapeDtypeStruct((16, inner), F32),
            jax.ShapeDtypeStruct((8, 128), F32),
        ),
        in_specs=[hbm] * 14,
        out_specs=[hbm] * 9,
        scratch_shapes=[
            pltpu.SMEM((1,), jnp.int32),
            vm((4, 1, inner), F32),
            vm((2, 1, own), F32),
            vm((16, inner), F32),
            vm((8, 128), F32),
            vm((padded, own), BF16),
            vm((NARROW - 1, padded, own), BF16),
            vm((padded, own), BF16),
            vm((2, own, full), BF16),
            vm((ntaps, full), BF16),
            vm((full, own), BF16),
            vm((padded, 128), F32),
            vm((4, wide, 8, 128), F32),
            vm((2, NARROW * wide, 8, 128), F32),
            vm((padded, 2 * inner), F32),
            vm((2, padded, 2 * inner), BF16),
            vm((2, padded, 2 * inner), BF16),
            vm((2, padded, inner), BF16),
            vm((2, padded, inner), BF16),
            vm((padded, inner), F32),
            vm((padded, inner), F32),
            vm((padded, inner), F32),
            vm(((dims[0] + 2) ** 2 * dims[1], inner), BF16),
            vm(((dims[2] + 2) ** 2 * dims[3], inner), BF16),
            vm((padded, ntaps), BF16),
            vm((padded, full), BF16),
            vm((padded, full), BF16),
            vm((padded, own), F32),
            vm((padded, own), BF16),
            vm((padded, full), BF16),
            vm((padded, full), BF16),
            vm((padded, ntaps), F32),
            vm((padded, full), BF16),
            vm((padded, own), BF16),
            vm((padded, own), BF16),
            vm((group, inner // group, NARROW * own), BF16),
            vm((NARROW, group, ntaps // group, inner), BF16),
            vm((2, group, own // 4, inner), BF16),
            vm((NARROW, inner // group, own), BF16),
            vm((group, NARROW, inner // group, own), BF16),
            vm((slots, NARROW, inner // group, own), BF16),
            vm((NARROW, group, ntaps // group, inner), BF16),
            vm((NARROW, slots, ntaps // group, inner), BF16),
            vm((2, group, inner, own // 4), BF16),
            vm((2, slots, inner, own // 4), BF16),
            pltpu.SemaphoreType.DMA((copies,)),
            pltpu.SemaphoreType.DMA((copies,)),
            pltpu.SemaphoreType.DMA((6,)),
            pltpu.SemaphoreType.DMA((6,)),
            pltpu.SemaphoreType.DMA((31,)),
        ],
        compiler_params=pltpu.CompilerParams(
            collective_id=0, has_side_effects=True, vmem_limit_bytes=62 * 2**20
        ),
    )(
        image_count,
        rows_first(views),
        rows_first(crops),
        rows_first(view_cot),
        rows_first(crop_cot),
        w_reduce,
        w_spatial.reshape(ntaps, full),
        w_expand,
        *(a.reshape(1, -1) for a in (gain_one, shift_one, gain_two, shift_two, gain_three, shift_three)),
    )
    shapes = [(outs[k].shape, BF16) for k in range(4)]
    shapes += [((NARROW * own, inner), F32), ((ntaps, full), F32), ((inner, NARROW * own), F32)]
    shapes += [((inner,), F32)] * 4 + [((own,), F32)] * 2
    outs = pl.pallas_call(
        release,
        name="release",
        out_shape=tuple(jax.ShapeDtypeStruct(*shape) for shape in shapes),
        in_specs=[hbm] * len(outs),
        out_specs=[hbm] * len(shapes),
        scratch_shapes=[
            vm(outs[4].shape, BF16),
            vm(outs[5].shape, BF16),
            vm(outs[6].shape, BF16),
            vm(shapes[4][0], F32),
            vm(shapes[5][0], F32),
            vm(shapes[6][0], F32),
            *[vm(outs[k].shape, BF16) for k in range(4)],
            vm(outs[7].shape, F32),
            vm(outs[8].shape, F32),
            pltpu.SemaphoreType.DMA((34,)),
        ],
        compiler_params=pltpu.CompilerParams(vmem_limit_bytes=62 * 2**20),
    )(*outs)
    images = (views, crops, views, crops)
    return (
        *(images_first(a, like) for a, like in zip(outs[:4], images)),
        outs[4],
        outs[5].reshape(w_spatial.shape),
        *outs[6:],
    )


def release(*refs):
    images, (reduce_in, spatial_in, expand_in, small, large) = refs[:4], refs[4:9]
    outs, (reduce_v, spatial_v, expand_v, reduce_f, spatial_f, expand_f, *staged, small_v, large_v, sems) = (
        refs[9:22],
        refs[22:],
    )
    used = [0]

    def copy(source, target):
        started = pltpu.make_async_copy(source, target, sems.at[used[0]])
        used[0] += 1
        started.start()
        return started

    loads = [copy(spatial_in, spatial_v), copy(expand_in, expand_v), copy(reduce_in, reduce_v)]
    arrivals = [copy(a, b) for a, b in zip(images, staged)]
    small_in, large_in = copy(small, small_v), copy(large, large_v)
    waits = []
    loads[0].wait()
    each = spatial_v.shape[1]
    for c in range(spatial_v.shape[0]):
        at = pl.ds(c * each, each)
        spatial_f[at] = spatial_v[c].astype(F32)
        if c % 2:
            pair = pl.ds((c - 1) * each, 2 * each)
            waits.append(copy(spatial_f.at[pair], outs[5].at[pair]))
    loads[1].wait()
    expand_f[...] = expand_v[...].astype(F32).reshape(expand_f.shape)
    waits.append(copy(expand_f, outs[6]))
    loads[2].wait()
    blocks, rows = reduce_v.shape[1:3]
    for k in range(2):
        for c in range(blocks):
            reduce_f[pl.ds((k * blocks + c) * rows, rows)] = reduce_v[k, c].astype(F32)
    waits.append(copy(reduce_f, outs[4]))
    for started, a, b in zip(arrivals, staged, outs[:4]):
        started.wait()
        waits.append(copy(a, b))
    small_in.wait()
    large_in.wait()
    for k, row in enumerate((0, 1, 8, 9)):
        waits.append(copy(small_v.at[row], outs[7 + k]))
    groups = large.shape[0] // 2
    for k in range(2):
        for g in range(groups):
            waits.append(copy(large_v.at[k * groups + g], outs[11 + k].at[pl.ds(128 * g, 128)]))
    for started in waits:
        started.wait()


def solution(mesh):
    wide = mesh.shape["wide"]
    image = P("wide", None, None, "narrow")
    vector = P("narrow")
    return jax.shard_map(
        functools.partial(per_device, wide),
        mesh=mesh,
        in_specs=(
            image, image, P("wide"), P(None, "narrow"), P(None, None, "narrow", None), P("narrow", None),
            vector, vector, vector, vector, vector, vector, image, image,
        ),
        out_specs=(
            image, image, image, image, P(None, "narrow"), P(None, None, "narrow", None),
            P("narrow", None), vector, vector, vector, vector, vector, vector,
        ),
        check_vma=False,
    )
```

profile of v0, /device:TPU:0, one launch (start us, length us, event | category | flops | bytes accessed | tf_op | source)
XLA Modules:
  0.0 136.2 jit_solution(10658708600128804207)
XLA Ops:
  1.3 130.4 %block.1 = (bf16[784,512]{1,0:T(8,128)(2,1)}, bf16[288,512]{1,0:T(8,128)(2,1)}, bf16[784,512]{1,0:T(8,128)(2,1)}, bf16[288,512]{1,0:T(8,128)(2,1)}, bf16[2,8,128...) custom-call(s32[1]{0:T(128)S(6)} %copy.27.refs_0_, ...), custom_call_target="tpu_custom_call" | custom-call | tf_op jit(solution)/shard_map/block/pallas_call | solution.py:892
  131.7 4.4 %release.1 = (bf16[784,512]{1,0:T(8,128)(2,1)}, bf16[288,512]{1,0:T(8,128)(2,1)}, bf16[784,512]{1,0:T(8,128)(2,1)}, bf16[288,512]{1,0:T(8,128)(2,1)}, f32[2048,1...) custom-call(bf16[784,512]{1,0:T(8,128)(2,1)} %get-tuple-element.35.r, ...), custom_call_target="tpu_custom_call" | custom-call | tf_op jit(solution)/shard_map/release/pallas_call | solution.py:977
where the time goes:
time: 136 us
  Pallas kernels  135 us (99%)
  between operations  1.46 us (1%)
    pallas_call x1, Pallas kernels, per_device(): pl.pallas_call(functools.partial(kernel, wide, dims), name='block', out_s...  130 us
    pallas_call x1, Pallas kernels, per_device(): pl.pallas_call(release, name='release', out_shape=tuple((jax.ShapeDtypeSt...  4.39 us

commit v1 on v0

--- a/solution.py
+++ b/solution.py
@@ -481,6 +481,19 @@
         for name in names:
             if name in tasks and next(tasks[name], "end") == "end":
                 del tasks[name]
+                write_out(name)
+
+    def write_out(name):
+        if name == "e":
+            results.append(local(out_e, expand_out))
+            return
+        k = int(name[1])
+        if name[0] == "s":
+            target = spatial_out.at[:, :, dyn_lanes(narrow_peer(k))]
+            results.append(local(out_s.at[k], target))
+        else:
+            target = reduce_out.at[q // 2 if k == 0 else 1 - q // 2]
+            results.append(local(out_r.at[k], target))
 
     for copy in load_reduce + load_x:
         copy.wait()
@@ -843,14 +856,8 @@
         local(dx.at[pl.ds(0, nview)], view_grad), local(dx.at[pl.ds(nview, rows - nview)], crop_grad)
     ]
     advance(*ORDER[3])
-    results.append(local(out_e, expand_out))
     while tasks:
         advance(*list(tasks))
-    results += [
-        local(out_s.at[p], spatial_out.at[:, :, dyn_lanes(narrow_peer(p))]) for p in range(NARROW)
-    ]
-    chip = q // 2
-    results += [local(out_r.at[0], reduce_out.at[chip]), local(out_r.at[1], reduce_out.at[1 - chip])]
     for copy in links.sent:
         copy.wait_send()
     for copy in pending:

time: 136 us -> 136 us (level)
  no operation moved by 1% of the time
where the time goes in v1:
time: 136 us
  Pallas kernels  134 us (99%)
  between operations  1.46 us (1%)
    pallas_call x1, Pallas kernels, per_device(): pl.pallas_call(functools.partial(kernel, wide, dims), name='block', out_s...  130 us
    pallas_call x1, Pallas kernels, per_device(): pl.pallas_call(release, name='release', out_shape=tuple((jax.ShapeDtypeSt...  4.39 us

profile of v1, /device:TPU:0, one launch (start us, length us, event | category | flops | bytes accessed | tf_op | source)
XLA Modules:
  0.0 135.5 jit_solution(12186025894443172953)
XLA Ops:
  1.3 129.7 %block.1 = (bf16[784,512]{1,0:T(8,128)(2,1)}, bf16[288,512]{1,0:T(8,128)(2,1)}, bf16[784,512]{1,0:T(8,128)(2,1)}, bf16[288,512]{1,0:T(8,128)(2,1)}, bf16[2,8,128...) custom-call(s32[1]{0:T(128)S(6)} %copy.27.refs_0_, ...), custom_call_target="tpu_custom_call" | custom-call | tf_op jit(solution)/shard_map/block/pallas_call | solution.py:899
  131.0 4.4 %release.1 = (bf16[784,512]{1,0:T(8,128)(2,1)}, bf16[288,512]{1,0:T(8,128)(2,1)}, bf16[784,512]{1,0:T(8,128)(2,1)}, bf16[288,512]{1,0:T(8,128)(2,1)}, f32[2048,1...) custom-call(bf16[784,512]{1,0:T(8,128)(2,1)} %get-tuple-element.35.r, ...), custom_call_target="tpu_custom_call" | custom-call | tf_op jit(solution)/shard_map/release/pallas_call | solution.py:984
